TPU v7x, 32 devices: a whole 2x2x4 slice. The times are simulated.
32 devices in a mesh: mp: 2 (over core), heads: 8 (over z, y), tok: 2 (over x).
Axes of the slice: x: 2, y: 2, z: 4, core: 2. Of those that a mesh axis runs over, the one named last changes fastest.
Arguments:
- context: bfloat16 [2, 512, 8192], P('mp', None, 'heads'), may hold values from -6 to 6
- out_weight: bfloat16 [2, 8192, 8192], P('mp', 'heads', 'tok'), may hold values from -0.0625 to 0.0625
- skip_states: bfloat16 [2, 512, 8192], P(None, None, 'tok'), may hold values from -6 to 6
- gram_old: float32 [8192, 8192], P('tok', ('mp', 'heads')), may hold values from -1 to 3
- cross_old: float32 [8192, 8192], P('tok', ('mp', 'heads')), may hold values from -30 to 30
- map_old: float32 [8192, 8192], P('tok', ('mp', 'heads')), may hold values from -0.3 to 0.3
Outputs:
- gram_new: float32 [8192, 8192], P('tok', ('mp', 'heads'))
- cross_new: float32 [8192, 8192], P('tok', ('mp', 'heads'))
- map_new: float32 [8192, 8192], P('tok', ('mp', 'heads'))
- residual_new: float32 [8192, 8192], P('tok', ('mp', 'heads'))
All inputs are finite; a program needn't handle non-finite values.
Results may differ from a plain program's by a relative error of at most 0.03.
Values may be sent and summed in bfloat16 or wider, within the bound.
A program may use at most 256 MiB of HBM per device.

v0:
```python
import jax
import jax.numpy as jnp
from jax import lax
from jax.sharding import PartitionSpec as P

decay_keep = 0.75
ridge_weight = 0.1


def from_root(block, axis, holder):
    block = jnp.where(lax.axis_index(axis) == holder, block, jnp.zeros_like(block))
    return lax.psum(block, axis)


def columns(matrix):
    return lax.all_gather(matrix, "tok", axis=0, tiled=True)


def token_inner(left, right):
    return lax.dot_general(
        left, right, (((0,), (0,)), ((), ())), preferred_element_type=jnp.float32
    )


def per_device(context, out_weight, skip_states, gram_old, cross_old, map_old):
    tokens = context.shape[1]
    width_a = gram_old.shape[0]
    width_c = gram_old.shape[1]
    partial_value = jnp.dot(context[0], out_weight[0], preferred_element_type=jnp.float32)
    model_index = lax.axis_index("mp")
    slot_mask = jnp.arange(2, dtype=jnp.int32) == model_index
    slot_terms = jnp.where(slot_mask[:, None, None], partial_value[None, :, :], 0.0)
    summed = lax.psum(slot_terms.astype(jnp.bfloat16), ("mp", "heads")).astype(jnp.float32)
    states = (summed + skip_states.astype(jnp.float32)).astype(jnp.bfloat16)
    source = states[0]
    target = states[1]
    column = lax.axis_index(("mp", "heads"))
    root_index = column * width_c // width_a
    offset = column * width_c - root_index * width_a
    picked = jnp.stack(
        [
            lax.dynamic_slice_in_dim(source, offset, width_c, 1),
            lax.dynamic_slice_in_dim(target, offset, width_c, 1),
        ]
    )
    fetched = from_root(picked, "tok", root_index)
    new_weight = (1.0 - decay_keep) / tokens
    gram_new = decay_keep * gram_old + new_weight * token_inner(source, fetched[0])
    cross_new = decay_keep * cross_old + new_weight * token_inner(source, fetched[1])
    gram_half = gram_new.astype(jnp.bfloat16)
    map_half = map_old.astype(jnp.bfloat16)
    row_panel = lax.all_gather(gram_half, ("mp", "heads"), axis=1, tiled=True)

    def apply_gram(matrix):
        return jnp.dot(row_panel, columns(matrix), preferred_element_type=jnp.float32)

    residual = cross_new - apply_gram(map_half) - ridge_weight * map_old
    applied = apply_gram(residual.astype(jnp.bfloat16)) + ridge_weight * residual
    totals = lax.psum(
        (jnp.sum(residual * residual), jnp.sum(residual * applied)), ("mp", "heads", "tok")
    )
    step_size = totals[0] / totals[1]
    return (gram_new, cross_new, map_old + step_size * residual, residual - step_size * applied)


def solution(mesh):
    placed = (
        P("mp", None, "heads"),
        P("mp", "heads", "tok"),
        P(None, None, "tok"),
        P("tok", ("mp", "heads")),
        P("tok", ("mp", "heads")),
        P("tok", ("mp", "heads")),
    )
    return jax.shard_map(
        per_device,
        mesh=mesh,
        in_specs=placed,
        out_specs=(
            P("tok", ("mp", "heads")),
            P("tok", ("mp", "heads")),
            P("tok", ("mp", "heads")),
            P("tok", ("mp", "heads")),
        ),
        check_vma=False,
    )
```

profile of v0, /device:TPU:0, one launch (start us, length us, event | category | flops | bytes accessed | tf_op | source)
XLA Modules:
  0.0 940.5 jit_solution(4489660221661309988)
XLA Ops:
  7.2 1.2 copy-done
  8.4 8.1 fusion
  16.5 5.4 select_convert_fusion
  21.9 0.0 all-reduce.6.cloned.1.call-start
  22.0 172.7 %all-reduce.4.cloned.1.call-done = bf16[2,512,4096]{2,1,0:T(8,128)(2,1)} async-done(((bf16[2,512,4096]{2,1,0:T(8,128)(2,1)}), bf16[2,512,4096]{2,1,0:T(8,128)(2,1)}) %all-reduce.4.cloned.1.call-update) | async-done | bytes 8388624 | tf_op jit(solution)/shard_map/psum | solution.py:33
  194.7 7.5 add_convert_fusion
  202.2 1.0 fusion.7
  203.3 2.4 copy-done.2
  205.6 0.1 constant_dynamic-slice_fusion
  205.7 1.1 maximum_select_fusion
  206.8 0.0 all-gather.6.cloned.1.call-start
  206.9 5.9 convert_element_type.26
  212.8 0.0 all-gather.4.cloned.1.call-start
  212.9 34.0 %all-reduce.6.cloned.1.call-done = bf16[2,512,512]{2,1,0:T(8,128)(2,1)} async-done(((bf16[2,512,512]{2,1,0:T(8,128)(2,1)}), bf16[2,512,512]{2,1,0:T(8,128)(2,1)}) %all-reduce.6.cloned.1.call-update) | async-done | bytes 1048592 | tf_op jit(solution)/shard_map/psum | solution.py:12
  246.9 13.9 %fusion.8 = (bf16[4096,512]{1,0:T(8,128)(2,1)}, f32[4096,512]{1,0:T(8,128)}) fusion(bf16[2,512,512]{2,1,0:T(8,128)(2,1)} %all-reduce.6.cloned.1.call-done, bf16[2,512,4096]{2,1,0:T(8,128)(2,1)} %copy-done.2, f32[4096,512]{1,0:T(8,128)} %param.9), kind=kOutput, calls=%fused_computation.24 | convolution fusion | flops 2155872256 | bytes 25690112 | tf_op jit(solution)/shard_map/dot_general | solution.py:20
  260.8 0.2 all-gather.8.cloned.1.call-start
  261.0 11.7 %multiply_add_fusion.2 = f32[4096,512]{1,0:T(8,128)} fusion(f32[4096,512]{1,0:T(8,128)} %param.10, bf16[2,512,512]{2,1,0:T(8,128)(2,1)S(1)} %copy-done.3, bf16[2,512,4096]{2,1,0:T(8,128)(2,1)} %copy-done.2), kind=kOutput, calls=%fused_computation.10 | convolution fusion | flops 2153775104 | bytes 21495808 | tf_op jit(solution)/shard_map/dot_general | solution.py:20
  272.7 79.7 %all-gather.6.cloned.1.call-done = bf16[8192,512]{1,0:T(8,128)(2,1)} async-done(((bf16[4096,512]{1,0:T(8,128)(2,1)}), bf16[8192,512]{1,0:T(8,128)(2,1)}) %all-gather.6.cloned.1.call-update) | async-done | bytes 8388624 | tf_op jit(solution)/shard_map/all_gather | solution.py:16
  352.5 328.2 %all-gather.4.cloned.1.call-done = bf16[4096,8192]{1,0:T(8,128)(2,1)} async-done(((bf16[4096,512]{1,0:T(8,128)(2,1)}), bf16[4096,8192]{1,0:T(8,128)(2,1)}) %all-gather.4.cloned.1.call-update) | async-done | bytes 67108880 | tf_op jit(solution)/shard_map/all_gather | solution.py:52
  680.7 47.0 %fusion.9 = (bf16[4096,512]{1,0:T(8,128)(2,1)}, f32[4096,512]{1,0:T(8,128)}) fusion(f32[4096,512]{1,0:T(8,128)} %param.11, f32[4096,512]{1,0:T(8,128)} %multiply_add_fusion.2, bf16[4096,8192]{1,0:T(8,128)(2,1)} %all-gather.4.cloned.1.call-done, bf16[8192,512]{1,0:T(8,128)(2,1)} %all-gather.6.cloned.1.call-done), kind=kOutput, calls=%fused_computation.25 | convolution fusion | flops 34368126976 | bytes 104857600 | tf_op jit(solution)/shard_map/dot_general | solution.py:55
  727.7 104.1 %all-gather.8.cloned.1.call-done = bf16[8192,512]{1,0:T(8,128)(2,1)} async-done(((bf16[4096,512]{1,0:T(8,128)(2,1)}), bf16[8192,512]{1,0:T(8,128)(2,1)}) %all-gather.8.cloned.1.call-update) | async-done | bytes 8388624 | tf_op jit(solution)/shard_map/all_gather | solution.py:16
  831.8 45.8 %multiply_reduce_fusion = (f32[]{:T(128)}, f32[]{:T(128)}, f32[4096,512]{1,0:T(8,128)}) fusion(f32[4096,512]{1,0:T(8,128)} %get-tuple-element.15, bf16[4096,8192]{1,0:T(8,128)(2,1)} %all-gather.4.cloned.1.call-done, bf16[8192,512]{1,0:T(8,128)(2,1)} %all-gather.8.cloned.1.call-done), kind=kOutput, calls=%fused_computation.6 | convolution fusion | flops 34372321280 | bytes 92274696 | tf_op jit(solution)/shard_map/dot_general | solution.py:55
  877.6 39.6 %all-reduce = (f32[]{:T(128)}, f32[]{:T(128)}) all-reduce(f32[]{:T(128)} %get-tuple-element.5, f32[]{:T(128)} %get-tuple-element.4), channel_id=1, replica_groups=mesh['mp'=2,'heads'=8,'tok'=2] {'mp','heads','tok'}, use_global_device_ids=true, to_apply=%region_3.4 | all-reduce | flops 2 | bytes 16 | tf_op jit(solution)/shard_map/psum | solution.py:59
  918.5 15.5 %multiply_subtract_fusion = (f32[4096,512]{1,0:T(8,128)}, f32[4096,512]{1,0:T(8,128)}) fusion(f32[4096,512]{1,0:T(8,128)} %get-tuple-element.15, f32[4096,512]{1,0:T(8,128)} %get-tuple-element.16, f32[]{:T(128)S(6)} %div.14, f32[4096,512]{1,0:T(8,128)} %param.11), kind=kLoop, calls=%fused_computation.4 | loop fusion | flops 12582912 | bytes 41943044 | tf_op jit(solution)/shard_map/sub | solution.py:63
  (13 shorter events, 0.1 us)
Async XLA Ops:
  7.2 1.2 copy-start
  7.2 187.5 %all-reduce.4.cloned.1.call-start = ((), (), s32[]{:S(2)}) async-start(), calls=%async_computation | async-start | bytes 16777216 | tf_op jit(solution)/shard_map/psum | solution.py:33
  21.9 224.9 %all-reduce.6.cloned.1.call-start = ((), (), s32[]{:S(2)}) async-start(), calls=%async_computation.1 | async-start | bytes 2097152 | tf_op jit(solution)/shard_map/psum | solution.py:12
  202.2 3.4 copy-start.2
  206.8 145.6 %all-gather.6.cloned.1.call-start = ((), (), s32[]{:S(2)}) async-start(), calls=%async_computation.3 | async-start | bytes 12582912 | tf_op jit(solution)/shard_map/all_gather | solution.py:16
  212.8 467.8 %all-gather.4.cloned.1.call-start = ((), (), s32[]{:S(2)}) async-start(), calls=%async_computation.2 | async-start | bytes 71303168 | tf_op jit(solution)/shard_map/all_gather | solution.py:52
  246.9 14.1 %copy-start.3 = (bf16[2,512,512]{2,1,0:T(8,128)(2,1)S(1)}, bf16[2,512,512]{2,1,0:T(8,128)(2,1)}, u32[]{:S(2)}) copy-start(bf16[2,512,512]{2,1,0:T(8,128)(2,1)} %all-reduce.6.cloned.1.call-done) | copy-start | bytes 3145732
  260.8 571.1 %all-gather.8.cloned.1.call-start = ((), (), s32[]{:S(2)}) async-start(), calls=%async_computation.4 | async-start | bytes 12582912 | tf_op jit(solution)/shard_map/all_gather | solution.py:16
  918.5 15.5 %copy-start.1 = (bf16[1,512,1024]{2,1,0:T(8,128)(2,1)S(1)}, bf16[1,512,1024]{2,1,0:T(8,128)(2,1)}, u32[]{:S(2)}) copy-start(bf16[1,512,1024]{2,1,0:T(8,128)(2,1)} %param.6) | copy-start | bytes 3145732
Sparse Core Ops, SparseCore 0:
  22.1 172.6 all-reduce.3
  207.0 39.8 all-reduce.5
  248.4 103.9 all-gather.5
  354.5 326.1 all-gather.3
  727.8 103.9 all-gather.7
where the time goes:
time: 941 us
  waiting for transfers between devices  719 us (76%)
  matrix products  126 us (13%)
  blocking collectives  39.6 us (4%)
  other arithmetic  35.4 us (4%)
  between operations  15.2 us (2%)
    all_gather x1, waiting for transfers between devices, per_device(): row_panel = lax.all_gather(gram_half, ('mp', 'heads'), axis=1, tiled=True)  328 us
    all_gather x2, waiting for transfers between devices, columns(): return lax.all_gather(matrix, 'tok', axis=0, tiled=True)  184 us
    psum x1, waiting for transfers between devices, per_device(): lax.psum(slot_terms.astype(jnp.bfloat16), ('mp', 'heads'))  173 us
    dot_general x2, matrix products, apply_gram(): jnp.dot(row_panel, columns(matrix), preferred_element_type=jnp.float32)  92.8 us
    psum x1, blocking collectives, per_device(): lax.psum((jnp.sum(residual * residual), jnp.sum(residual * applied)), ('m...  39.6 us
    psum x1, waiting for transfers between devices, from_root(): return lax.psum(block, axis)  34 us
    dot_general x2, matrix products, token_inner(): lax.dot_general(left, right, (((0,), (0,)), ((), ())), preferred_element_...  25.6 us
  transfers between devices with their start and end apart: 5, of which 5 were waited for; matrix products, arithmetic and copies ran while one was open for 3% of the time, Pallas kernels for 0%

commit v1 on v0

--- a/solution.py
+++ b/solution.py
@@ -57,7 +57,8 @@
     residual = cross_new - apply_gram(map_half) - ridge_weight * map_old
     applied = apply_gram(residual.astype(jnp.bfloat16)) + ridge_weight * residual
     totals = lax.psum(
-        (jnp.sum(residual * residual), jnp.sum(residual * applied)), ("mp", "heads", "tok")
+        lax.psum((jnp.sum(residual * residual), jnp.sum(residual * applied)), ("heads", "tok")),
+        "mp",
     )
     step_size = totals[0] / totals[1]
     return (gram_new, cross_new, map_old + step_size * residual, residual - step_size * applied)

time: 941 us -> 946 us (level)
    psum x1 -> x2, blocking collectives: 39.6 us -> 44.6 us  [the longest x1 41.4 us: per_device(): lax.psum((jnp.sum(residual * residual), jnp.sum(residual * applied)), ('h...]
where the time goes in v1:
time: 946 us
  waiting for transfers between devices  719 us (76%)
  matrix products  126 us (13%)
  blocking collectives  44.6 us (5%)
  other arithmetic  35.4 us (4%)
  between operations  15.2 us (2%)
    all_gather x1, waiting for transfers between devices, per_device(): row_panel = lax.all_gather(gram_half, ('mp', 'heads'), axis=1, tiled=True)  328 us
    all_gather x2, waiting for transfers between devices, columns(): return lax.all_gather(matrix, 'tok', axis=0, tiled=True)  184 us
    psum x1, waiting for transfers between devices, per_device(): lax.psum(slot_terms.astype(jnp.bfloat16), ('mp', 'heads'))  173 us
    dot_general x2, matrix products, apply_gram(): jnp.dot(row_panel, columns(matrix), preferred_element_type=jnp.float32)  92.8 us
    psum x1, blocking collectives, per_device(): lax.psum((jnp.sum(residual * residual), jnp.sum(residual * applied)), ('h...  41.4 us
    psum x1, waiting for transfers between devices, from_root(): return lax.psum(block, axis)  34 us
    dot_general x2, matrix products, token_inner(): lax.dot_general(left, right, (((0,), (0,)), ((), ())), preferred_element_...  25.6 us
  transfers between devices with their start and end apart: 5, of which 5 were waited for; matrix products, arithmetic and copies ran while one was open for 3% of the time, Pallas kernels for 0%

profile of v1, /device:TPU:0, one launch (start us, length us, event | category | flops | bytes accessed | tf_op | source)
XLA Modules:
  0.0 945.5 jit_solution(16316702799474717400)
XLA Ops:
  7.2 1.2 copy-done
  8.4 8.1 fusion
  16.5 5.4 select_convert_fusion
  22.0 172.7 %all-reduce.5.cloned.1.call-done = bf16[2,512,4096]{2,1,0:T(8,128)(2,1)} async-done(((bf16[2,512,4096]{2,1,0:T(8,128)(2,1)}), bf16[2,512,4096]{2,1,0:T(8,128)(2,1)}) %all-reduce.5.cloned.1.call-update) | async-done | bytes 8388624 | tf_op jit(solution)/shard_map/psum | solution.py:33
  194.7 7.5 add_convert_fusion
  202.2 1.0 fusion.7
  203.3 2.4 copy-done.2
  205.6 0.1 constant_dynamic-slice_fusion
  205.7 1.1 maximum_select_fusion
  206.8 0.0 all-gather.6.cloned.1.call-start
  206.9 5.9 convert_element_type.26
  212.8 0.0 all-gather.4.cloned.1.call-start
  212.9 34.0 %all-reduce.7.cloned.1.call-done = bf16[2,512,512]{2,1,0:T(8,128)(2,1)} async-done(((bf16[2,512,512]{2,1,0:T(8,128)(2,1)}), bf16[2,512,512]{2,1,0:T(8,128)(2,1)}) %all-reduce.7.cloned.1.call-update) | async-done | bytes 1048592 | tf_op jit(solution)/shard_map/psum | solution.py:12
  246.9 13.9 %fusion.8 = (bf16[4096,512]{1,0:T(8,128)(2,1)}, f32[4096,512]{1,0:T(8,128)}) fusion(bf16[2,512,512]{2,1,0:T(8,128)(2,1)} %all-reduce.7.cloned.1.call-done, bf16[2,512,4096]{2,1,0:T(8,128)(2,1)} %copy-done.2, f32[4096,512]{1,0:T(8,128)} %param.9), kind=kOutput, calls=%fused_computation.24 | convolution fusion | flops 2155872256 | bytes 25690112 | tf_op jit(solution)/shard_map/dot_general | solution.py:20
  260.8 0.2 all-gather.8.cloned.1.call-start
  261.0 11.7 %multiply_add_fusion.2 = f32[4096,512]{1,0:T(8,128)} fusion(f32[4096,512]{1,0:T(8,128)} %param.10, bf16[2,512,512]{2,1,0:T(8,128)(2,1)S(1)} %copy-done.3, bf16[2,512,4096]{2,1,0:T(8,128)(2,1)} %copy-done.2), kind=kOutput, calls=%fused_computation.10 | convolution fusion | flops 2153775104 | bytes 21495808 | tf_op jit(solution)/shard_map/dot_general | solution.py:20
  272.7 79.7 %all-gather.6.cloned.1.call-done = bf16[8192,512]{1,0:T(8,128)(2,1)} async-done(((bf16[4096,512]{1,0:T(8,128)(2,1)}), bf16[8192,512]{1,0:T(8,128)(2,1)}) %all-gather.6.cloned.1.call-update) | async-done | bytes 8388624 | tf_op jit(solution)/shard_map/all_gather | solution.py:16
  352.5 328.2 %all-gather.4.cloned.1.call-done = bf16[4096,8192]{1,0:T(8,128)(2,1)} async-done(((bf16[4096,512]{1,0:T(8,128)(2,1)}), bf16[4096,8192]{1,0:T(8,128)(2,1)}) %all-gather.4.cloned.1.call-update) | async-done | bytes 67108880 | tf_op jit(solution)/shard_map/all_gather | solution.py:52
  680.7 47.0 %fusion.9 = (bf16[4096,512]{1,0:T(8,128)(2,1)}, f32[4096,512]{1,0:T(8,128)}) fusion(f32[4096,512]{1,0:T(8,128)} %param.11, f32[4096,512]{1,0:T(8,128)} %multiply_add_fusion.2, bf16[4096,8192]{1,0:T(8,128)(2,1)} %all-gather.4.cloned.1.call-done, bf16[8192,512]{1,0:T(8,128)(2,1)} %all-gather.6.cloned.1.call-done), kind=kOutput, calls=%fused_computation.25 | convolution fusion | flops 34368126976 | bytes 104857600 | tf_op jit(solution)/shard_map/dot_general | solution.py:55
  727.7 104.1 %all-gather.8.cloned.1.call-done = bf16[8192,512]{1,0:T(8,128)(2,1)} async-done(((bf16[4096,512]{1,0:T(8,128)(2,1)}), bf16[8192,512]{1,0:T(8,128)(2,1)}) %all-gather.8.cloned.1.call-update) | async-done | bytes 8388624 | tf_op jit(solution)/shard_map/all_gather | solution.py:16
  831.8 45.8 %multiply_reduce_fusion = (f32[]{:T(128)}, f32[]{:T(128)}, f32[4096,512]{1,0:T(8,128)}) fusion(f32[4096,512]{1,0:T(8,128)} %get-tuple-element.17, bf16[4096,8192]{1,0:T(8,128)(2,1)} %all-gather.4.cloned.1.call-done, bf16[8192,512]{1,0:T(8,128)(2,1)} %all-gather.8.cloned.1.call-done), kind=kOutput, calls=%fused_computation.6 | convolution fusion | flops 34372321280 | bytes 92274696 | tf_op jit(solution)/shard_map/dot_general | solution.py:55
  877.6 41.4 %all-reduce = (f32[]{:T(128)}, f32[]{:T(128)}) all-reduce(f32[]{:T(128)} %get-tuple-element.5, f32[]{:T(128)} %get-tuple-element.4), channel_id=1, replica_groups=mesh['mp'=2,'heads'=8,'tok'=2] {'heads','tok'}, use_global_device_ids=true, to_apply=%region_3.4 | all-reduce | flops 2 | bytes 16 | tf_op jit(solution)/shard_map/psum | solution.py:60
  919.1 3.1 all-reduce.1
  923.5 15.5 %multiply_subtract_fusion = (f32[4096,512]{1,0:T(8,128)}, f32[4096,512]{1,0:T(8,128)}) fusion(f32[4096,512]{1,0:T(8,128)} %get-tuple-element.17, f32[4096,512]{1,0:T(8,128)} %get-tuple-element.18, f32[]{:T(128)S(6)} %div.14, f32[4096,512]{1,0:T(8,128)} %param.11), kind=kLoop, calls=%fused_computation.4 | loop fusion | flops 12582912 | bytes 41943044 | tf_op jit(solution)/shard_map/sub | solution.py:64
  (14 shorter events, 0.2 us)
Async XLA Ops:
  7.2 1.2 copy-start
  7.2 187.5 %all-reduce.5.cloned.1.call-start = ((), (), s32[]{:S(2)}) async-start(), calls=%async_computation | async-start | bytes 16777216 | tf_op jit(solution)/shard_map/psum | solution.py:33
  21.9 224.9 %all-reduce.7.cloned.1.call-start = ((), (), s32[]{:S(2)}) async-start(), calls=%async_computation.1 | async-start | bytes 2097152 | tf_op jit(solution)/shard_map/psum | solution.py:12
  202.2 3.4 copy-start.2
  206.8 145.6 %all-gather.6.cloned.1.call-start = ((), (), s32[]{:S(2)}) async-start(), calls=%async_computation.3 | async-start | bytes 12582912 | tf_op jit(solution)/shard_map/all_gather | solution.py:16
  212.8 467.8 %all-gather.4.cloned.1.call-start = ((), (), s32[]{:S(2)}) async-start(), calls=%async_computation.2 | async-start | bytes 71303168 | tf_op jit(solution)/shard_map/all_gather | solution.py:52
  246.9 14.1 %copy-start.3 = (bf16[2,512,512]{2,1,0:T(8,128)(2,1)S(1)}, bf16[2,512,512]{2,1,0:T(8,128)(2,1)}, u32[]{:S(2)}) copy-start(bf16[2,512,512]{2,1,0:T(8,128)(2,1)} %all-reduce.7.cloned.1.call-done) | copy-start | bytes 3145732
  260.8 571.1 %all-gather.8.cloned.1.call-start = ((), (), s32[]{:S(2)}) async-start(), calls=%async_computation.4 | async-start | bytes 12582912 | tf_op jit(solution)/shard_map/all_gather | solution.py:16
  923.5 15.5 %copy-start.1 = (bf16[1,512,1024]{2,1,0:T(8,128)(2,1)S(1)}, bf16[1,512,1024]{2,1,0:T(8,128)(2,1)}, u32[]{:S(2)}) copy-start(bf16[1,512,1024]{2,1,0:T(8,128)(2,1)} %param.6) | copy-start | bytes 3145732
Sparse Core Ops, SparseCore 0:
  22.1 172.6 all-reduce.4
  207.0 39.8 all-reduce.6
  248.4 103.9 all-gather.5
  354.5 326.1 all-gather.3
  727.8 103.9 all-gather.7
